TPU v7x, 128 devices: a whole 4x4x4 slice. The times are simulated.
128 devices in a mesh: expert: 8 (over y, core), dp: 16 (over x, z).
Axes of the slice: x: 4, y: 4, z: 4, core: 2. Of those that a mesh axis runs over, the one named last changes fastest.
Arguments:
- tokens: bfloat16 [512, 4096], P(('expert', 'dp')), may hold values from -6 to 6
- gate_weight: bfloat16 [4096, 28672], P(('expert', 'dp')), may hold values from -0.09375 to 0.09375
- up_weight: bfloat16 [4096, 28672], P(('expert', 'dp')), may hold values from -0.09375 to 0.09375
- down_weight_t: bfloat16 [4096, 28672], P(('expert', 'dp')), may hold values from -0.03125 to 0.03125
- router: bfloat16 [4096, 16], replicated, may hold values from -0.25 to 0.25
- cluster_ids: int32 [224], replicated, may hold values from 0 to 15, as said below
Outputs:
- residual: bfloat16 [512, 4096], P(('expert', 'dp'))
- grad_down: bfloat16 [4096, 28672], P(('expert', 'dp'))
Inputs may be any that keep to these rules, and one draw needn't show every extreme that they name: `cluster_ids`: every expert holds one block or more. Experts e * 2 to e * 2 + 1 form group e; no group holds more than 64 blocks, and exactly one group holds that many.
All inputs are finite; a program needn't handle non-finite values.
Results may differ from a plain program's by a relative error of at most 0.0064.
Values may be sent and summed in bfloat16 or wider, within the bound.
A program may use at most 128 MiB of HBM per device.

v0:
```python
import jax
import jax.numpy as jnp
from jax import lax
from jax.sharding import PartitionSpec as P

D = 4096
FF = 28672
BLOCK = 128
EXP_DEV = 2


def per_device(tokens, gate_weight, up_weight, down_weight_t, router, cluster_ids):
    expert_count = lax.axis_size("expert")
    dp_count = lax.axis_size("dp")
    devices = expert_count * dp_count
    block_count = FF // BLOCK
    d_local = gate_weight.shape[0]
    row_count = tokens.shape[0]
    total_rows = row_count * devices
    block_ids = jnp.arange(block_count, dtype=jnp.int32)
    even_share = -(-block_count // devices)
    slot_count = 2 * even_share
    group_of = cluster_ids // EXP_DEV
    member = group_of[None, :] == jnp.arange(expert_count, dtype=jnp.int32)[:, None]
    running_rank = jnp.cumsum(member.astype(jnp.int32), axis=1) - 1
    group_rank = jnp.sum(jnp.where(member, running_rank, 0), axis=0)
    device_of = group_of * dp_count + group_rank % dp_count
    slot_of = group_rank // dp_count
    target = device_of * slot_count + slot_of
    matches = target[None, :] == jnp.arange(devices * slot_count, dtype=jnp.int32)[:, None]
    block_table = jnp.sum(jnp.where(matches, block_ids[None, :], 0), axis=1)
    is_valid = jnp.any(matches, axis=1)

    def pick_columns(weight_rows):
        blocked = weight_rows.reshape(d_local, block_count, BLOCK)
        picked = jnp.take(blocked, block_table, axis=1)
        picked = jnp.where(is_valid[None, :, None], picked, jnp.zeros_like(picked))
        return picked.reshape(d_local, devices, slot_count, BLOCK)

    gate_in, up_in, down_in = (
        lax.all_to_all(
            pick_columns(gate_weight), ("expert", "dp"), split_axis=1, concat_axis=0, tiled=True
        ),
        lax.all_to_all(
            pick_columns(up_weight), ("expert", "dp"), split_axis=1, concat_axis=0, tiled=True
        ),
        lax.all_to_all(
            pick_columns(down_weight_t), ("expert", "dp"), split_axis=1, concat_axis=0, tiled=True
        ),
    )
    width_here = slot_count * BLOCK
    gate_mine = gate_in.reshape(D, width_here)
    up_mine = up_in.reshape(D, width_here)
    down_mine = down_in.reshape(D, width_here)
    own_index = lax.axis_index(("expert", "dp"))
    own_blocks = lax.dynamic_slice_in_dim(block_table, own_index * slot_count, slot_count)
    own_experts = jnp.take(cluster_ids, own_blocks)
    router_cols = jnp.take(router, own_experts, axis=1)
    shard_rows = lax.all_gather(tokens, ("expert", "dp"), axis=0, tiled=True)
    gate_pre = jnp.dot(shard_rows, gate_mine, preferred_element_type=jnp.float32)
    up_pre = jnp.dot(shard_rows, up_mine, preferred_element_type=jnp.float32)
    hidden = jax.nn.silu(gate_pre) * up_pre
    logits = jnp.dot(shard_rows, router_cols, preferred_element_type=jnp.float32)
    gate_scale = jnp.repeat(2.0 * jax.nn.sigmoid(logits) - 1.0, BLOCK, axis=1)
    scaled = (gate_scale * hidden).astype(jnp.bfloat16)
    inv_root = 1.0 / float(total_rows) ** 0.5
    row_block = scaled
    residual_f = lax.psum_scatter(
        lax.dot_general(
            row_block, down_mine, (((1,), (1,)), ((), ())), preferred_element_type=jnp.float32
        ),
        ("expert", "dp"),
        scatter_dimension=0,
        tiled=True,
    )
    residual = residual_f.astype(jnp.bfloat16)
    row_block = scaled
    grad_f = lax.dot_general(
        lax.all_gather(residual, ("expert", "dp"), axis=0, tiled=True),
        row_block,
        (((0,), (0,)), ((), ())),
        preferred_element_type=jnp.float32,
    )
    grad_blocks = (grad_f * inv_root).astype(jnp.bfloat16).reshape(D, 1, slot_count, BLOCK)
    returned = lax.all_to_all(
        grad_blocks, ("expert", "dp"), split_axis=0, concat_axis=1, tiled=True
    )
    returned = returned.reshape(d_local, devices * slot_count, BLOCK)
    placement = matches.astype(jnp.bfloat16)
    placed = jnp.einsum("dkc,kb->dbc", returned, placement, preferred_element_type=jnp.float32)
    grad_down = placed.astype(jnp.bfloat16).reshape(d_local, FF)
    return (residual, grad_down)


def solution(mesh):
    in_specs = (
        P(("expert", "dp"), None),
        P(("expert", "dp"), None),
        P(("expert", "dp"), None),
        P(("expert", "dp"), None),
        P(),
        P(),
    )
    out_specs = (P(("expert", "dp"), None), P(("expert", "dp"), None))
    return jax.shard_map(
        per_device, mesh=mesh, in_specs=in_specs, out_specs=out_specs, check_vma=False
    )
```

profile of v0, /device:TPU:1, one launch (start us, length us, event | category | flops | bytes accessed | tf_op | source)
XLA Modules:
  0.0 524.1 jit_solution(11179238339386088591)
XLA Ops:
  7.2 0.8 and_select_fusion.3
  8.0 0.6 reduce-window.6
  8.6 0.2 slice_reduce_fusion
  9.0 0.8 fusion.40
  9.8 0.1 select_reduce_fusion
  9.9 0.1 fusion.31
  10.1 1.5 copy_bitcast_fusion.3
  11.6 0.3 copy_bitcast_fusion.2
  12.0 4.6 gather_fusion.2
  16.6 3.5 gather_fusion.3
  20.1 1.8 copy_bitcast_fusion.1
  21.9 3.5 gather_fusion.4
  25.4 9.2 %bitcast_select_fusion = (bf16[32,512,128]{2,0,1:T(8,128)(2,1)}, bf16[32,512,128]{2,0,1:T(8,128)(2,1)}, bf16[32,512,128]{2,0,1:T(8,128)(2,1)S(1)}) fusion(bf16[512,32,128]{2,1,0:T(8,128)(2,1)} %gather_fusion.4, pred[512]{0:T(512)(128)(4,1)S(1)} %compare_and_fusion, pred[512]{0:T(512)(128)(4,1)S(1)} %fusion.31, bf16[512,32,128]{2,1,0:T(8,128)(2,1)} %gather_fusion.3, ...), kind=kLoop, calls=%fused_computation.15 | loop fusion | flops 12582912 | bytes 25166848 | tf_op jit(solution)/shard_map/jit(_where)/select_n | solution.py:37
  34.6 6.2 %copy.32 = bf16[32,128,4,128]{3,2,0,1:T(4,128)(2,1)} copy(bf16[32,128,4,128]{3,0,2,1:T(8,128)(2,1)S(1)} %bitcast.104) | data formatting | bytes 8388608 | tf_op jit(solution)/shard_map/reshape | solution.py:38
  40.7 12.0 %all-to-all-start = ((bf16[32,128,4,128]{3,2,0,1:T(4,128)(2,1)}), bf16[32,128,4,128]{3,2,0,1:T(4,128)(2,1)}, u32[]{:S(2)}, u32[]{:S(2)}) async-start(bf16[32,128,4,128]{3,2,0,1:T(4,128)(2,1)} %copy.32), calls=%async_computation | async-start | bytes 8388608 | tf_op jit(solution)/shard_map/all_to_all | solution.py:41
  52.7 0.5 all-gather.5.cloned.1.call-start
  53.2 0.2 all-gather.5.cloned.1.call-update
  53.4 8.3 %copy.34 = bf16[32,128,4,128]{3,2,0,1:T(4,128)(2,1)} copy(bf16[32,128,4,128]{3,0,2,1:T(8,128)(2,1)} %bitcast.103) | data formatting | bytes 8388608 | tf_op jit(solution)/shard_map/reshape | solution.py:38
  61.8 43.4 %all-to-all-done = bf16[32,128,4,128]{3,2,0,1:T(4,128)(2,1)} async-done(((bf16[32,128,4,128]{3,2,0,1:T(4,128)(2,1)}), bf16[32,128,4,128]{3,2,0,1:T(4,128)(2,1)}, u32[]{:S(2)}, u32[]{:S(2)}) %all-to-all-start) | async-done | bytes 4194336 | tf_op jit(solution)/shard_map/all_to_all | solution.py:41
  105.2 5.1 all-to-all-start.1
  110.2 8.4 %copy.36 = bf16[32,128,4,128]{3,2,0,1:T(4,128)(2,1)} copy(bf16[32,128,4,128]{3,0,2,1:T(8,128)(2,1)} %bitcast.102) | data formatting | bytes 8388608 | tf_op jit(solution)/shard_map/reshape | solution.py:38
  118.6 45.1 %all-to-all-done.1 = bf16[32,128,4,128]{3,2,0,1:T(4,128)(2,1)} async-done(((bf16[32,128,4,128]{3,2,0,1:T(4,128)(2,1)}), bf16[32,128,4,128]{3,2,0,1:T(4,128)(2,1)}, u32[]{:S(2)}, u32[]{:S(2)}) %all-to-all-start.1) | async-done | bytes 4194336 | tf_op jit(solution)/shard_map/all_to_all | solution.py:44
  163.8 5.0 all-to-all-start.2
  168.8 0.2 all-gather.7.cloned.1.call-start
  169.0 0.1 compare_select_fusion.2
  169.1 0.6 gather_fusion
  169.7 0.1 compare_and_fusion.1
  169.8 0.6 gather_fusion.1
  170.4 46.4 %all-gather.5.cloned.1.call-done = bf16[128,4,4096]{2,1,0:T(4,128)(2,1)} async-done(((bf16[1,4,4096]{2,1,0:T(4,128)(2,1)}), bf16[128,4,4096]{2,1,0:T(4,128)(2,1)}) %all-gather.5.cloned.1.call-update) | async-done | bytes 4194320 | tf_op jit(solution)/shard_map/all_gather | solution.py:59
  216.9 6.9 %reshape.142 = bf16[512,4096]{1,0:T(8,128)(2,1)} reshape(bf16[128,4,4096]{2,1,0:T(4,128)(2,1)} %all-gather.5.cloned.1.call-done) | data formatting | bytes 8388608
  223.8 3.5 fusion.29
  227.3 4.6 fusion.9
  232.0 0.1 broadcast_in_dim.70
  232.1 4.8 fusion.21
  236.9 7.8 %fusion = f32[512,4096]{1,0:T(8,128)} fusion(bf16[512,512]{0,1:T(8,128)(2,1)S(1)} %fusion.21, bf16[512,8,4,128]{3,2,1,0:T(4,128)(2,1)} %bitcast.46), kind=kOutput, calls=%fused_computation.6 | convolution fusion | flops 2147483648 | bytes 13107200 | tf_op jit(solution)/shard_map/dot_general | solution.py:69
  244.7 118.3 %all-reduce.3 = bf16[512,4096]{1,0:T(8,128)(2,1)} all-reduce(f32[512,4096]{1,0:T(8,128)} %fusion), channel_id=2, replica_groups=mesh['expert'=8,'dp'=16] {'expert','dp'}, use_global_device_ids=true, to_apply=%region_5.7.clone | all-reduce | flops 2097152 | bytes 12582912
  363.0 1.5 fusion.49
  364.5 64.6 %all-gather.7.cloned.1.call-done = bf16[128,4,4096]{2,1,0:T(4,128)(2,1)} async-done(((bf16[1,4,4096]{2,1,0:T(4,128)(2,1)}), bf16[128,4,4096]{2,1,0:T(4,128)(2,1)}) %all-gather.7.cloned.1.call-update) | async-done | bytes 4194320 | tf_op jit(solution)/shard_map/all_gather | solution.py:79
  429.1 6.9 %reshape.144 = bf16[512,4096]{1,0:T(8,128)(2,1)} reshape(bf16[128,4,4096]{2,1,0:T(4,128)(2,1)} %all-gather.7.cloned.1.call-done) | data formatting | bytes 8388608
  436.0 6.5 %multiply_convert_fusion = bf16[4096,512]{0,1:T(8,128)(2,1)} fusion(bf16[512,512]{0,1:T(8,128)(2,1)S(1)} %fusion.21, bf16[512,4096]{1,0:T(8,128)(2,1)} %reshape.144), kind=kOutput, calls=%fused_computation.5 | convolution fusion | flops 2151677952 | bytes 8912896 | tf_op jit(solution)/shard_map/dot_general | solution.py:78
  442.5 7.5 %copy.37 = bf16[4096,1,4,128]{3,2,1,0:T(4,128)(2,1)} copy(bf16[4096,1,4,128]{0,3,2,1:T(8,128)(2,1)} %bitcast.107) | data formatting | bytes 8388608 | tf_op jit(solution)/shard_map/reshape | solution.py:84
  450.0 5.8 %all-to-all-start.3 = ((bf16[4096,1,4,128]{3,2,1,0:T(4,128)(2,1)}), bf16[4096,1,4,128]{3,2,1,0:T(4,128)(2,1)}, u32[]{:S(2)}, u32[]{:S(2)}) async-start(bf16[4096,1,4,128]{3,2,1,0:T(4,128)(2,1)} %copy.37), calls=%async_computation.3 | async-start | bytes 8388608 | tf_op jit(solution)/shard_map/all_to_all | solution.py:85
  455.8 1.5 dynamic-slice_convert_fusion
  457.3 50.6 %all-to-all-done.3 = bf16[4096,1,4,128]{3,2,1,0:T(4,128)(2,1)} async-done(((bf16[4096,1,4,128]{3,2,1,0:T(4,128)(2,1)}), bf16[4096,1,4,128]{3,2,1,0:T(4,128)(2,1)}, u32[]{:S(2)}, u32[]{:S(2)}) %all-to-all-start.3) | async-done | bytes 4194336 | tf_op jit(solution)/shard_map/all_to_all | solution.py:85
  507.9 2.7 copy.38
  510.6 3.2 copy.39
  513.9 1.2 convolution_convert_fusion
  515.1 1.9 copy.73
  (25 shorter events, 0.2 us)
Async XLA Ops:
  7.2 2.9 copy-start
  8.9 2.8 copy-start.5
  40.7 64.4 %all-to-all-start = ((bf16[32,128,4,128]{3,2,0,1:T(4,128)(2,1)}), bf16[32,128,4,128]{3,2,0,1:T(4,128)(2,1)}, u32[]{:S(2)}, u32[]{:S(2)}) async-start(bf16[32,128,4,128]{3,2,0,1:T(4,128)(2,1)} %copy.32), calls=%async_computation | async-start | bytes 8388608 | tf_op jit(solution)/shard_map/all_to_all | solution.py:41
  52.7 164.2 %all-gather.5.cloned.1.call-start = ((), (), s32[]{:S(2)}) async-start(), calls=%async_computation.4 | async-start | bytes 4227072 | tf_op jit(solution)/shard_map/all_gather | solution.py:59
  105.2 58.6 %all-to-all-start.1 = ((bf16[32,128,4,128]{3,2,0,1:T(4,128)(2,1)}), bf16[32,128,4,128]{3,2,0,1:T(4,128)(2,1)}, u32[]{:S(2)}, u32[]{:S(2)}) async-start(bf16[32,128,4,128]{3,2,0,1:T(4,128)(2,1)} %copy.34), calls=%async_computation.1 | async-start | bytes 8388608 | tf_op jit(solution)/shard_map/all_to_all | solution.py:44
  118.6 50.5 %copy-start.3 = (s32[224]{0:T(256)S(1)}, s32[224]{0:T(256)}, u32[]{:S(2)}) copy-start(s32[224]{0:T(256)} %param.13) | copy-start | bytes 2692
  118.6 51.2 %copy-start.2 = (bf16[4096,16]{0,1:T(8,128)(2,1)S(1)}, bf16[4096,16]{0,1:T(8,128)(2,1)}, u32[]{:S(2)}) copy-start(bf16[4096,16]{0,1:T(8,128)(2,1)} %param.12) | copy-start | bytes 393220
  163.8 73.1 %all-to-all-start.2 = ((bf16[32,128,4,128]{3,2,0,1:T(4,128)(2,1)}), bf16[32,128,4,128]{3,2,0,1:T(4,128)(2,1)}, u32[]{:S(2)}, u32[]{:S(2)}) async-start(bf16[32,128,4,128]{3,2,0,1:T(4,128)(2,1)} %copy.36), calls=%async_computation.2 | async-start | bytes 8388608 | tf_op jit(solution)/shard_map/all_to_all | solution.py:47
  168.8 260.3 %all-gather.7.cloned.1.call-start = ((), (), s32[]{:S(2)}) async-start(), calls=%async_computation.5 | async-start | bytes 4227072 | tf_op jit(solution)/shard_map/all_gather | solution.py:79
  223.8 3.5 copy-start.4
  450.0 57.9 %all-to-all-start.3 = ((bf16[4096,1,4,128]{3,2,1,0:T(4,128)(2,1)}), bf16[4096,1,4,128]{3,2,1,0:T(4,128)(2,1)}, u32[]{:S(2)}, u32[]{:S(2)}) async-start(bf16[4096,1,4,128]{3,2,1,0:T(4,128)(2,1)} %copy.37), calls=%async_computation.3 | async-start | bytes 8388608 | tf_op jit(solution)/shard_map/all_to_all | solution.py:85
  513.9 3.2 copy-start.1
Sparse Core Ops, SparseCore 0:
  56.7 160.1 all-gather.4
  364.6 64.4 all-gather.6
where the time goes:
time: 532 us; the launch traced here: 524 us
  waiting for transfers between devices  250 us (47%)
  blocking collectives  118 us (22%)
  local copies, waits for them, and re-layouts  71.9 us (14%)
  starting transfers between devices  28.5 us (5%)
  matrix products  28.5 us (5%)
  between operations  14.5 us (3%)
  other arithmetic  12 us (2%)
    unnamed x1, blocking collectives  118 us
    all_gather x1, waiting for transfers between devices, per_device(): lax.all_gather(residual, ('expert', 'dp'), axis=0, tiled=True)  64.6 us
    all_to_all x1, waiting for transfers between devices, per_device(): lax.all_to_all(grad_blocks, ('expert', 'dp'), split_axis=0, concat_axis=1...  50.6 us
    all_gather x1, waiting for transfers between devices, per_device(): shard_rows = lax.all_gather(tokens, ('expert', 'dp'), axis=0, tiled=True)  46.4 us
    all_to_all x1, waiting for transfers between devices, per_device(): lax.all_to_all(pick_columns(up_weight), ('expert', 'dp'), split_axis=1, c...  45.1 us
    all_to_all x1, waiting for transfers between devices, per_device(): lax.all_to_all(pick_columns(gate_weight), ('expert', 'dp'), split_axis=1,...  43.4 us
    reshape x3, local copies, waits for them, and re-layouts, pick_columns(): return picked.reshape(d_local, devices, slot_count, BLOCK)  22.9 us
    unnamed x16, local copies, waits for them, and re-layouts  17.3 us
  transfers between devices with their start and end apart: 6, of which 5 were waited for; matrix products, arithmetic and copies ran while one was open for 8% of the time, Pallas kernels for 0%

commit v1 on v0

v1 whole, which is shorter than its diff:
```python
import jax
import jax.numpy as jnp
from jax import lax
from jax.experimental import pallas as pl
from jax.experimental.pallas import tpu as pltpu
from jax.sharding import PartitionSpec as P

MESH = pl.DeviceIdType.MESH
BF = jnp.bfloat16
F32 = jnp.float32

D = 4096
FF = 28672
EXPERTS = 16
BLOCK = 128
TOKENS = 512
NY = 4
ND = 16
ROWS = 32
KD = D // NY
FD = FF // ND
FC = FD // 2
CHUNKS = (2, 2, 3)
STARTS = (0, 2, 4)
H = 2
RH = ROWS // H
IH = ND * RH
TQ = TOKENS // NY
INV_ROOT = 1.0 / float(TOKENS) ** 0.5


def local_copy(src, dst, sem):
    return pltpu.make_async_copy(src, dst, sem)


def wait_bytes(ref, sem):
    pltpu.make_async_copy(ref, ref, sem).wait()


def kernel(
    tok, gw, uw, dw, router, ids,
    resid_out, grad_out,
    tok_send, tok_recv, tokens, wrecv, part, psum, logit, lsum, s, wd, p, rr, rfull, out16, gs,
    tok_s, w_s, w_r, p_s, p_r, l_s, l_r, s_s, s_r, d_s, d_r, rp_s, rp_r, ra_s, ra_r, o_s, o_r, g_s, g_r,
):
    e = lax.axis_index("expert")
    d = lax.axis_index("dp")
    y, c = e // 2, e % 2
    x, z = d // 4, d % 4

    def plane_peer(o):
        return ((x + o // 4) % 4) * 4 + (z + o % 4) % 4

    def remote(src, dst, ssem, rsem, te, td):
        pltpu.make_async_remote_copy(
            src, dst, ssem, rsem, device_id=(te, td), device_id_type=MESH
        ).start()

    def each(lo, hi, body):
        def step(o, carry):
            body(o)
            return carry

        lax.fori_loop(lo, hi, step, 0)

    bar = pltpu.get_barrier_semaphore()

    def greet_plane(o):
        pl.semaphore_signal(
            bar, inc=1, device_id=(y * 2 + (c + o % 2) % 2, plane_peer(o // 2)), device_id_type=MESH
        )

    each(1, 32, greet_plane)

    def greet_others(o):
        y2 = (y + 1 + o // 2) % 4
        pl.semaphore_signal(bar, inc=1, device_id=(y2 * 2 + o % 2, d), device_id_type=MESH)

    each(0, 6, greet_others)

    t = tok[...].astype(F32)
    t16 = jnp.concatenate([t] * 4, axis=0)
    row = lax.broadcasted_iota(jnp.int32, t16.shape, 0)
    t16 = jnp.where(row // 4 == y, t16, 0.0).astype(BF)
    for k in range(NY):
        tok_send[k] = t16[:, k * KD : (k + 1) * KD]

    pl.semaphore_wait(bar, 37)

    def send_tok_col(o):
        y2 = (y + o) % 4
        remote(tok_send.at[y2], tok_recv.at[o - 1], tok_s.at[0], tok_s.at[1], y2 * 2 + c, d)

    each(1, NY, send_tok_col)

    def issue_gu(m, k):
        w = (gw, uw)[m]
        n, first = CHUNKS[k], STARTS[k]
        me = c * ND + d

        def cols(c2, d2):
            return pl.ds(pl.multiple_of(d2 * FD + c2 * FC + first * BLOCK, BLOCK), n * BLOCK)

        def body(o):
            c2, d2 = (c + o % 2) % 2, plane_peer(o // 2)
            remote(w.at[:, cols(c2, d2)], wrecv[k].at[m, me], w_s.at[m, k], w_r.at[m, k], y * 2 + c2, d2)

        each(1, 32, body)
        local_copy(w.at[:, cols(c, d)], wrecv[k].at[m, me], w_r.at[m, k]).start()

    def issue_down(h):
        def cols(d2):
            return pl.ds(pl.multiple_of(d2 * FD, BLOCK), FD)

        rows = pl.ds(h * RH, RH)

        def body(o):
            d2 = plane_peer(o)
            remote(dw.at[rows, cols(d2)], wd.at[h, d], d_s.at[h], d_r.at[h], e, d2)

        each(1, ND, body)
        local_copy(dw.at[rows, cols(d)], wd.at[h, d], d_r.at[h]).start()

    issue_gu(0, 0)

    wait_bytes(tok_recv, tok_s.at[1])
    mine = tok_send[y].astype(F32)
    for k in range(NY - 1):
        mine = mine + tok_recv[k].astype(F32)
    tokens[d, c] = mine.astype(BF)

    def send_tok_plane(o):
        remote(tokens.at[d, c], tokens.at[d, c], tok_s.at[2], tok_s.at[3], e, plane_peer(o))

    each(1, ND, send_tok_plane)
    issue_gu(1, 0)
    issue_gu(0, 1)
    wait_bytes(tokens.at[pl.ds(0, ND - 1), 0], tok_s.at[3])
    remote(tokens.at[:, c], tokens.at[:, c], tok_s.at[4], tok_s.at[5], y * 2 + 1 - c, d)
    issue_gu(1, 1)
    wait_bytes(tokens.at[:, 0], tok_s.at[5])
    rows_all = tokens[...].reshape(TOKENS, KD)

    logit[...] = jnp.zeros_like(logit)
    logit[:, :EXPERTS] = jnp.dot(
        rows_all, router[pl.ds(pl.multiple_of(y * KD, KD), KD), :], preferred_element_type=F32
    )

    def rows_of(y2):
        return pl.ds(pl.multiple_of(y2 * TQ, TQ), TQ)

    def send_logit(o):
        y2 = (y + o) % 4
        remote(logit.at[rows_of(y2)], lsum.at[o - 1], l_s, l_r, y2 * 2 + c, d)

    each(1, NY, send_logit)

    def partial(k):
        n = CHUNKS[k]
        for m in range(2):
            wait_bytes(wrecv[k].at[m], w_r.at[m, k])
            got = wrecv[k][m].reshape(KD, n * BLOCK)
            part[k][m] = jnp.dot(rows_all, got, preferred_element_type=F32).astype(BF)

            def send(o):
                y2 = (y + o) % 4
                remote(part[k].at[m, rows_of(y2)], psum[k].at[m, o - 1], p_s.at[m, k], p_r.at[m, k], y2 * 2 + c, d)

            each(1, NY, send)

    def hidden(k):
        n, first = CHUNKS[k], STARTS[k]
        for m in range(2):
            wait_bytes(psum[k].at[m], p_r.at[m, k])
        sums = []
        for m in range(2):
            total = part[k][m, rows_of(y)].astype(F32)
            for o in range(NY - 1):
                total = total + psum[k][m, o].astype(F32)
            sums.append(total)
        lane = lax.broadcasted_iota(jnp.int32, (TQ, EXPERTS), 1)
        for j in range(n):
            expert = ids[d * (FD // BLOCK) + c * (FC // BLOCK) + first + j]
            scale = jnp.sum(jnp.where(lane == expert, gate_scale, 0.0), axis=1, keepdims=True)
            g = sums[0][:, j * BLOCK : (j + 1) * BLOCK]
            u = sums[1][:, j * BLOCK : (j + 1) * BLOCK]
            col = (first + j) * BLOCK
            s[c, rows_of(y), col : col + BLOCK] = (scale * (g * jax.nn.sigmoid(g) * u)).astype(BF)
        view = s.at[c, rows_of(y), pl.ds(first * BLOCK, n * BLOCK)]

        def send(o):
            remote(view, view, s_s.at[k], s_r.at[k], (e + o) % 8, d)

        each(1, 8, send)

    partial(0)
    issue_gu(0, 2)
    issue_gu(1, 2)
    partial(1)
    issue_down(0)

    wait_bytes(lsum, l_r)
    total = logit[rows_of(y), :EXPERTS]
    for o in range(NY - 1):
        total = total + lsum[o][:, :EXPERTS]
    gate_scale = 2.0 * jax.nn.sigmoid(total) - 1.0
    hidden(0)
    partial(2)
    issue_down(1)
    hidden(1)
    hidden(2)
    for k in range(3):
        wait_bytes(sview(s, k), s_r.at[k])

    def residual(h):
        wait_bytes(wd.at[h], d_r.at[h])
        w = wd[h].reshape(IH, FD)
        acc = lax.dot_general(s[0], w[:, :FC], (((1,), (1,)), ((), ())), preferred_element_type=F32)
        acc = acc + lax.dot_general(s[1], w[:, FC:], (((1,), (1,)), ((), ())), preferred_element_type=F32)
        p[h] = acc.astype(BF).reshape(ND, 32, IH)

        def send(o):
            d2 = plane_peer(o)
            remote(p.at[h, d2], rr.at[h, o - 1], rp_s.at[h], rp_r.at[h], e, d2)

        each(1, ND, send)

    def reduce_residual(h):
        wait_bytes(rr.at[h], rp_r.at[h])
        acc = p[h, d].astype(F32)
        for o in range(ND - 1):
            acc = acc + rr[h, o].astype(F32)
        rfull[h, d] = acc.astype(BF)
        view = rfull.at[h, d]

        def send(o):
            remote(view, view, ra_s.at[h], ra_r.at[h], e, plane_peer(o))

        each(1, ND, send)

        def send_out(o):
            e2 = (e + o) % 8
            rows = pl.ds(pl.multiple_of((e2 % 2) * 16, 16), 16)
            remote(rfull.at[h, d, rows], out16.at[e, h], o_s.at[h], o_r.at[h], e2, d)

        each(1, 8, send_out)
        rows = pl.ds(pl.multiple_of(c * 16, 16), 16)
        local_copy(rfull.at[h, d, rows], out16.at[e, h], o_r.at[h]).start()

    def gradient(h):
        wait_bytes(rfull.at[h, pl.ds(0, ND - 1)], ra_r.at[h])
        r = rfull[h].reshape(TOKENS, IH)
        for c2 in range(2):
            g = lax.dot_general(r, s[c2], (((0,), (0,)), ((), ())), preferred_element_type=F32)
            gs[h, :, :, c2 * FC : (c2 + 1) * FC] = (g * INV_ROOT).astype(BF).reshape(ND, RH, FC)
        rows = pl.ds(h * RH, RH)
        cols = pl.ds(pl.multiple_of(d * FD, BLOCK), FD)

        def send(o):
            d2 = plane_peer(o)
            remote(gs.at[h, d2], grad_out.at[rows, cols], g_s.at[h], g_r.at[h], e, d2)

        each(1, ND, send)
        local_copy(gs.at[h, d], grad_out.at[rows, cols], g_r.at[h]).start()

    residual(0)
    residual(1)
    reduce_residual(0)
    reduce_residual(1)
    gradient(0)
    gradient(1)

    for h in range(H):
        wait_bytes(out16.at[:, h], o_r.at[h])
    both = jnp.concatenate([out16[:, h].reshape(8 * 16, IH) for h in range(H)], axis=1)
    src = lax.broadcasted_iota(jnp.int32, (H * IH, H * IH), 0)
    dst = lax.broadcasted_iota(jnp.int32, (H * IH, H * IH), 1)
    place = (dst // ROWS) * RH + ((dst % ROWS) // RH) * IH + dst % RH
    order = jnp.where(src == place, 1.0, 0.0).astype(BF)
    ordered = jnp.dot(both, order, preferred_element_type=F32)
    for k in range(8):
        rows16 = ordered[k * 16 : (k + 1) * 16]
        pick = jnp.where(y == 0, rows16[0:4], 0.0)
        for y2 in range(1, NY):
            pick = jnp.where(y == y2, rows16[4 * y2 : 4 * y2 + 4], pick)
        resid_out[:, k * H * IH : (k + 1) * H * IH] = pick.astype(BF)

    wait_bytes(tok_recv, tok_s.at[0])
    wait_bytes(tokens.at[pl.ds(0, ND - 1), 0], tok_s.at[2])
    wait_bytes(tokens.at[:, 0], tok_s.at[4])
    wait_bytes(lsum, l_s)
    for k in range(3):
        for m in range(2):
            wait_bytes(wrecv[k].at[m, pl.ds(0, 31)], w_s.at[m, k])
            wait_bytes(psum[k].at[m], p_s.at[m, k])
        wait_bytes(sview(s, k), s_s.at[k])
    for h in range(H):
        wait_bytes(wd.at[h, pl.ds(0, ND - 1)], d_s.at[h])
        wait_bytes(rr.at[h], rp_s.at[h])
        wait_bytes(rfull.at[h, pl.ds(0, ND - 1)], ra_s.at[h])
        wait_bytes(out16.at[pl.ds(0, 7), h], o_s.at[h])
        wait_bytes(gs.at[h, pl.ds(0, ND - 1)], g_s.at[h])
        wait_bytes(grad_out.at[pl.ds(h * RH, RH)], g_r.at[h])


def sview(s, k):
    return s.at[0, pl.ds(0, 7 * 64), pl.ds(0, 2 * CHUNKS[k] * BLOCK)]


def per_device(tokens, gate_weight, up_weight, down_weight_t, router, cluster_ids):
    dma = pltpu.SemaphoreType.DMA
    nk = len(CHUNKS)
    hbm = pl.BlockSpec(memory_space=pl.ANY)
    vmem = pl.BlockSpec(memory_space=pltpu.VMEM)
    smem = pl.BlockSpec(memory_space=pltpu.SMEM)
    return pl.pallas_call(
        kernel,
        out_shape=(
            jax.ShapeDtypeStruct((TOKENS // 128, D), BF),
            jax.ShapeDtypeStruct((ROWS, FF), BF),
        ),
        in_specs=[vmem, hbm, hbm, hbm, vmem, smem],
        out_specs=(vmem, hbm),
        scratch_shapes=[
            pltpu.VMEM((NY, 16, KD), BF),
            pltpu.VMEM((NY - 1, 16, KD), BF),
            pltpu.VMEM((ND, 2, 16, KD), BF),
            tuple(pltpu.VMEM((2, 32, ROWS, n * BLOCK), BF) for n in CHUNKS),
            tuple(pltpu.VMEM((2, TOKENS, n * BLOCK), BF) for n in CHUNKS),
            tuple(pltpu.VMEM((2, NY - 1, TQ, n * BLOCK), BF) for n in CHUNKS),
            pltpu.VMEM((TOKENS, 128), F32),
            pltpu.VMEM((NY - 1, TQ, 128), F32),
            pltpu.VMEM((2, TOKENS, FC), BF),
            pltpu.VMEM((H, ND, RH, FD), BF),
            pltpu.VMEM((H, ND, 32, IH), BF),
            pltpu.VMEM((H, ND - 1, 32, IH), BF),
            pltpu.VMEM((H, ND, 32, IH), BF),
            pltpu.VMEM((8, H, 16, IH), BF),
            pltpu.VMEM((H, ND, RH, FD), BF),
            dma((6,)),
            dma((2, nk)), dma((2, nk)),
            dma((2, nk)), dma((2, nk)),
            dma, dma,
            dma((nk,)), dma((nk,)),
            dma((H,)), dma((H,)),
            dma((H,)), dma((H,)),
            dma((H,)), dma((H,)),
            dma((H,)), dma((H,)),
            dma((H,)), dma((H,)),
        ],
        compiler_params=pltpu.CompilerParams(
            collective_id=0, has_side_effects=True, vmem_limit_bytes=48 * 2**20
        ),
    )(tokens, gate_weight, up_weight, down_weight_t, router, cluster_ids)


def solution(mesh):
    split = P(("expert", "dp"), None)
    return jax.shard_map(
        per_device,
        mesh=mesh,
        in_specs=(split, split, split, split, P(), P()),
        out_specs=(split, split),
        check_vma=False,
    )
```

time: 532 us -> 130 us (0.24); the launches traced: 524 us -> 130 us
  waiting for transfers between devices: 250 us -> 0 us
  Pallas kernels: 0 us -> 123 us
  blocking collectives: 118 us -> 0 us
  local copies, waits for them, and re-layouts: 71.9 us -> 6.16 us
  matrix products: 28.5 us -> 0 us
  starting transfers between devices: 28.5 us -> 0 us
  between operations: 14.5 us -> 0.66 us
  other arithmetic: 12 us -> 0 us
    all_to_all x4 -> x0, waiting for transfers between devices: 139 us -> none  [the longest x1 50.6 us: per_device(): lax.all_to_all(grad_blocks, ('expert', 'dp'), split_axis=0, concat_axis=1...]
    pallas_call x0 -> x1, Pallas kernels: none -> 123 us  [per_device(): pl.pallas_call(kernel, out_shape=(jax.ShapeDtypeStruct((TOKENS // 128, D)...]
    unnamed x1 -> x0, blocking collectives: 118 us -> none
    all_gather x2 -> x0, waiting for transfers between devices: 111 us -> none  [the longest x1 64.6 us: per_device(): lax.all_gather(residual, ('expert', 'dp'), axis=0, tiled=True)]
    reshape x7 -> x0, local copies, waits for them, and re-layouts: 34.1 us -> none  [the longest x3 22.9 us: pick_columns(): return picked.reshape(d_local, devices, slot_count, BLOCK)]
    dot_general x6 -> x0, matrix products: 28.5 us -> none  [the longest x1 7.8 us: per_device(): lax.dot_general(row_block, down_mine, (((1,), (1,)), ((), ())), preferred...]
    all_to_all x4 -> x0, starting transfers between devices: 27.8 us -> none  [the longest x1 12 us: per_device(): lax.all_to_all(pick_columns(gate_weight), ('expert', 'dp'), split_axis=1,...]
    gather x5 -> x0, local copies, waits for them, and re-layouts: 12.8 us -> none  [the longest x3 11.6 us: pick_columns(): picked = jnp.take(blocked, block_table, axis=1)]
  transfers between devices with their start and end apart: 6 -> 0, of which waited for: 5 -> 0; matrix products, arithmetic and copies ran while one was open for 8% -> 0% of each run, Pallas kernels for 0% -> 0%
where the time goes in v1:
time: 130 us
  Pallas kernels  123 us (95%)
  local copies, waits for them, and re-layouts  6.16 us (5%)
    pallas_call x1, Pallas kernels, per_device(): pl.pallas_call(kernel, out_shape=(jax.ShapeDtypeStruct((TOKENS // 128, D)...  123 us
    unnamed x9, local copies, waits for them, and re-layouts  6.16 us

profile of v1, /device:TPU:1, one launch (start us, length us, event | category | flops | bytes accessed | tf_op | source)
XLA Modules:
  0.0 130.1 jit_solution(3661078697042364105)
XLA Ops:
  0.6 1.4 %copy.8.router = bf16[4096,16]{1,0:T(8,128)(2,1)S(1)} copy(bf16[4096,16]{0,1:T(8,128)(2,1)} %param.10) | data formatting | bytes 262144 | tf_op args[4]
  2.0 0.0 copy-start
  2.0 1.5 %copy-done = bf16[32,28672]{1,0:T(8,128)(2,1)S(1)} copy-done((bf16[32,28672]{1,0:T(8,128)(2,1)S(1)}, bf16[32,28672]{1,0:T(8,128)(2,1)}, u32[]{:S(2)}) %copy-start) | copy-done | bytes 1835032
  3.5 0.0 copy-start.1
  3.5 0.8 copy-done.1
  4.3 0.0 copy-start.2
  4.3 0.7 copy-done.2
  5.0 123.3 %shard_map.77 = (bf16[4,4096]{1,0:T(4,128)(2,1)S(1)}, bf16[32,28672]{1,0:T(8,128)(2,1)S(1)}) custom-call(bf16[4,4096]{1,0:T(4,128)(2,1)S(1)} %copy-done.1, bf16[32,28672]{1,0:T(8,128)(2,1)S(1)} %copy-done, bf16[32,28672]{1,0:T(8,128)(2,1)} %uw.1, bf16[32,28672]{1,0:T(8,128)(2,1)} %dw.1, bf16[4096,16]{1,0:T(8,128)(2,1)S(1)} %copy.8.router, s32[224]{0:T(256)S(1)} %copy-done.2), custom_call_target="tpu_custom_call" | custom-call | tf_op jit(solution)/shard_map/pallas_call | solution.py:316
  128.3 0.6 copy.11
  128.9 1.2 copy.12
Async XLA Ops:
  2.0 1.5 %copy-start = (bf16[32,28672]{1,0:T(8,128)(2,1)S(1)}, bf16[32,28672]{1,0:T(8,128)(2,1)}, u32[]{:S(2)}) copy-start(bf16[32,28672]{1,0:T(8,128)(2,1)} %gw.1) | copy-start | bytes 5505028
  3.5 0.8 copy-start.1
  4.3 0.7 copy-start.2

commit v2 on v1

--- a/solution.py
+++ b/solution.py
@@ -20,12 +20,19 @@
 KD = D // NY
 FD = FF // ND
 FC = FD // 2
-CHUNKS = (2, 2, 3)
-STARTS = (0, 2, 4)
+CHUNKS = (2, 2, 2, 1)
+STARTS = (0, 2, 4, 6)
+NK = len(CHUNKS)
+SENT = ((F32, BF), (F32, BF), (F32, BF), (F32, BF))
 H = 2
 RH = ROWS // H
 IH = ND * RH
 TQ = TOKENS // NY
+PLAN = (
+    ("I", 0, 2), ("I", 1, 2), ("P", 0, 0), ("P", 1, 0), ("I", 0, 3), ("I", 1, 3), ("D", 0), ("D", 1), ("L",),
+    ("P", 0, 1), ("P", 1, 1), ("H", 0), ("P", 0, 2), ("P", 1, 2), ("H", 1), ("F", 0),
+    ("P", 0, 3), ("P", 1, 3), ("H", 2), ("F", 1), ("H", 3), ("F", 2), ("F", 3),
+)
 INV_ROOT = 1.0 / float(TOKENS) ** 0.5
 
 
@@ -38,10 +45,10 @@
 
 
 def kernel(
-    tok, gw, uw, dw, router, ids,
+    tok_in, gw, uw, dw, router_in, ids,
     resid_out, grad_out,
-    tok_send, tok_recv, tokens, wrecv, part, psum, logit, lsum, s, wd, p, rr, rfull, out16, gs,
-    tok_s, w_s, w_r, p_s, p_r, l_s, l_r, s_s, s_r, d_s, d_r, rp_s, rp_r, ra_s, ra_r, o_s, o_r, g_s, g_r,
+    tok, router, tok_send, tok_recv, tokens, wrecv, part, own, psum, logit, lsum, s, wd, p, rr, rfull, out16, gs,
+    in_s, tok_s, w_s, w_r, p_s, p_r, l_s, l_r, s_s, s_r, f_s, f_r, d_s, d_r, rp_s, rp_r, ra_s, ra_r, o_s, o_r, g_s, g_r,
 ):
     e = lax.axis_index("expert")
     d = lax.axis_index("dp")
@@ -63,6 +70,13 @@
 
         lax.fori_loop(lo, hi, step, 0)
 
+    tok_copy = local_copy(tok_in, tok, in_s.at[0])
+    tok_copy.start()
+    router_copy = local_copy(
+        router_in.at[:, pl.ds(pl.multiple_of(y * KD, KD), KD)], router, in_s.at[1]
+    )
+    router_copy.start()
+
     bar = pltpu.get_barrier_semaphore()
 
     def greet_plane(o):
@@ -78,6 +92,7 @@
 
     each(0, 6, greet_others)
 
+    tok_copy.wait()
     t = tok[...].astype(F32)
     t16 = jnp.concatenate([t] * 4, axis=0)
     row = lax.broadcasted_iota(jnp.int32, t16.shape, 0)
@@ -141,9 +156,10 @@
     wait_bytes(tokens.at[:, 0], tok_s.at[5])
     rows_all = tokens[...].reshape(TOKENS, KD)
 
+    router_copy.wait()
     logit[...] = jnp.zeros_like(logit)
-    logit[:, :EXPERTS] = jnp.dot(
-        rows_all, router[pl.ds(pl.multiple_of(y * KD, KD), KD), :], preferred_element_type=F32
+    logit[:, :EXPERTS] = lax.dot_general(
+        rows_all, router[...], (((1,), (1,)), ((), ())), preferred_element_type=F32
     )
 
     def rows_of(y2):
@@ -155,28 +171,35 @@
 
     each(1, NY, send_logit)
 
-    def partial(k):
+    def partial(m, k):
         n = CHUNKS[k]
-        for m in range(2):
-            wait_bytes(wrecv[k].at[m], w_r.at[m, k])
-            got = wrecv[k][m].reshape(KD, n * BLOCK)
-            part[k][m] = jnp.dot(rows_all, got, preferred_element_type=F32).astype(BF)
-
-            def send(o):
-                y2 = (y + o) % 4
-                remote(part[k].at[m, rows_of(y2)], psum[k].at[m, o - 1], p_s.at[m, k], p_r.at[m, k], y2 * 2 + c, d)
-
-            each(1, NY, send)
+        wait_bytes(wrecv[k].at[m], w_r.at[m, k])
+        got = wrecv[k][m].reshape(KD, n * BLOCK)
+        dot = jnp.dot(rows_all, got, preferred_element_type=F32)
+        if SENT[k][m] == F32:
+            part[k][m][...] = dot
+        else:
+            part[k][m][...] = dot.astype(BF)
+            own[k][m][...] = dot
+
+        def send(o):
+            y2 = (y + o) % 4
+            remote(part[k][m].at[rows_of(y2)], psum[k][m].at[o - 1], p_s.at[m, k], p_r.at[m, k], y2 * 2 + c, d)
+
+        each(1, NY, send)
+
+    def step_cols(k):
+        return pl.ds(STARTS[k] * BLOCK, CHUNKS[k] * BLOCK)
 
     def hidden(k):
         n, first = CHUNKS[k], STARTS[k]
-        for m in range(2):
-            wait_bytes(psum[k].at[m], p_r.at[m, k])
         sums = []
         for m in range(2):
-            total = part[k][m, rows_of(y)].astype(F32)
+            wait_bytes(psum[k][m], p_r.at[m, k])
+            kept = part[k][m] if SENT[k][m] == F32 else own[k][m]
+            total = kept[rows_of(y)]
             for o in range(NY - 1):
-                total = total + psum[k][m, o].astype(F32)
+                total = total + psum[k][m][o].astype(F32)
             sums.append(total)
         lane = lax.broadcasted_iota(jnp.int32, (TQ, EXPERTS), 1)
         for j in range(n):
@@ -186,31 +209,37 @@
             u = sums[1][:, j * BLOCK : (j + 1) * BLOCK]
             col = (first + j) * BLOCK
             s[c, rows_of(y), col : col + BLOCK] = (scale * (g * jax.nn.sigmoid(g) * u)).astype(BF)
-        view = s.at[c, rows_of(y), pl.ds(first * BLOCK, n * BLOCK)]
-
-        def send(o):
-            remote(view, view, s_s.at[k], s_r.at[k], (e + o) % 8, d)
-
-        each(1, 8, send)
-
-    partial(0)
-    issue_gu(0, 2)
-    issue_gu(1, 2)
-    partial(1)
-    issue_down(0)
-
-    wait_bytes(lsum, l_r)
-    total = logit[rows_of(y), :EXPERTS]
-    for o in range(NY - 1):
-        total = total + lsum[o][:, :EXPERTS]
-    gate_scale = 2.0 * jax.nn.sigmoid(total) - 1.0
-    hidden(0)
-    partial(2)
-    issue_down(1)
-    hidden(1)
-    hidden(2)
-    for k in range(3):
-        wait_bytes(sview(s, k), s_r.at[k])
+        view = s.at[c, rows_of(y), step_cols(k)]
+
+        def send(o):
+            remote(view, view, s_s.at[k], s_r.at[k], (y + o) % 4 * 2 + c, d)
+
+        each(1, NY, send)
+
+    def hand_over(k):
+        wait_bytes(s.at[0, pl.ds(0, 3 * TQ), step_cols(k)], s_r.at[k])
+        view = s.at[c, :, step_cols(k)]
+        remote(view, view, f_s.at[k], f_r.at[k], y * 2 + 1 - c, d)
+
+    for op in PLAN:
+        if op[0] == "I":
+            issue_gu(*op[1:])
+        elif op[0] == "D":
+            issue_down(op[1])
+        elif op[0] == "P":
+            partial(*op[1:])
+        elif op[0] == "L":
+            wait_bytes(lsum, l_r)
+            total = logit[rows_of(y), :EXPERTS]
+            for o in range(NY - 1):
+                total = total + lsum[o][:, :EXPERTS]
+            gate_scale = 2.0 * jax.nn.sigmoid(total) - 1.0
+        elif op[0] == "H":
+            hidden(op[1])
+        else:
+            hand_over(op[1])
+    for k in range(NK):
+        wait_bytes(s.at[0, :, step_cols(k)], f_r.at[k])
 
     def residual(h):
         wait_bytes(wd.at[h], d_r.at[h])
@@ -289,11 +318,12 @@
     wait_bytes(tokens.at[pl.ds(0, ND - 1), 0], tok_s.at[2])
     wait_bytes(tokens.at[:, 0], tok_s.at[4])
     wait_bytes(lsum, l_s)
-    for k in range(3):
+    for k in range(NK):
         for m in range(2):
             wait_bytes(wrecv[k].at[m, pl.ds(0, 31)], w_s.at[m, k])
-            wait_bytes(psum[k].at[m], p_s.at[m, k])
-        wait_bytes(sview(s, k), s_s.at[k])
+            wait_bytes(psum[k][m], p_s.at[m, k])
+        wait_bytes(s.at[0, pl.ds(0, 3 * TQ), step_cols(k)], s_s.at[k])
+        wait_bytes(s.at[0, :, step_cols(k)], f_s.at[k])
     for h in range(H):
         wait_bytes(wd.at[h, pl.ds(0, ND - 1)], d_s.at[h])
         wait_bytes(rr.at[h], rp_s.at[h])
@@ -303,14 +333,10 @@
         wait_bytes(grad_out.at[pl.ds(h * RH, RH)], g_r.at[h])
 
 
-def sview(s, k):
-    return s.at[0, pl.ds(0, 7 * 64), pl.ds(0, 2 * CHUNKS[k] * BLOCK)]
-
-
 def per_device(tokens, gate_weight, up_weight, down_weight_t, router, cluster_ids):
     dma = pltpu.SemaphoreType.DMA
-    nk = len(CHUNKS)
-    hbm = pl.BlockSpec(memory_space=pl.ANY)
+    nk = NK
+    hbm = pl.BlockSpec(memory_space=pltpu.HBM)
     vmem = pl.BlockSpec(memory_space=pltpu.VMEM)
     smem = pl.BlockSpec(memory_space=pltpu.SMEM)
     return pl.pallas_call(
@@ -319,15 +345,18 @@
             jax.ShapeDtypeStruct((TOKENS // 128, D), BF),
             jax.ShapeDtypeStruct((ROWS, FF), BF),
         ),
-        in_specs=[vmem, hbm, hbm, hbm, vmem, smem],
-        out_specs=(vmem, hbm),
+        in_specs=[hbm, hbm, hbm, hbm, hbm, smem],
+        out_specs=(vmem, pl.BlockSpec(memory_space=pl.ANY)),
         scratch_shapes=[
+            pltpu.VMEM((TOKENS // 128, D), BF),
+            pltpu.VMEM((EXPERTS, KD), BF),
             pltpu.VMEM((NY, 16, KD), BF),
             pltpu.VMEM((NY - 1, 16, KD), BF),
             pltpu.VMEM((ND, 2, 16, KD), BF),
             tuple(pltpu.VMEM((2, 32, ROWS, n * BLOCK), BF) for n in CHUNKS),
-            tuple(pltpu.VMEM((2, TOKENS, n * BLOCK), BF) for n in CHUNKS),
-            tuple(pltpu.VMEM((2, NY - 1, TQ, n * BLOCK), BF) for n in CHUNKS),
+            tuple(tuple(pltpu.VMEM((TOKENS, n * BLOCK), t) for t in ts) for n, ts in zip(CHUNKS, SENT)),
+            tuple(tuple(pltpu.VMEM((TOKENS, n * BLOCK), F32) for _ in range(2)) for n in CHUNKS),
+            tuple(tuple(pltpu.VMEM((NY - 1, TQ, n * BLOCK), t) for t in ts) for n, ts in zip(CHUNKS, SENT)),
             pltpu.VMEM((TOKENS, 128), F32),
             pltpu.VMEM((NY - 1, TQ, 128), F32),
             pltpu.VMEM((2, TOKENS, FC), BF),
@@ -337,11 +366,13 @@
             pltpu.VMEM((H, ND, 32, IH), BF),
             pltpu.VMEM((8, H, 16, IH), BF),
             pltpu.VMEM((H, ND, RH, FD), BF),
+            dma((2,)),
             dma((6,)),
             dma((2, nk)), dma((2, nk)),
             dma((2, nk)), dma((2, nk)),
             dma, dma,
             dma((nk,)), dma((nk,)),
+            dma((nk,)), dma((nk,)),
             dma((H,)), dma((H,)),
             dma((H,)), dma((H,)),
             dma((H,)), dma((H,)),
@@ -349,9 +380,9 @@
             dma((H,)), dma((H,)),
         ],
         compiler_params=pltpu.CompilerParams(
-            collective_id=0, has_side_effects=True, vmem_limit_bytes=48 * 2**20
+            collective_id=0, has_side_effects=True, vmem_limit_bytes=54 * 2**20
         ),
-    )(tokens, gate_weight, up_weight, down_weight_t, router, cluster_ids)
+    )(tokens, gate_weight, up_weight, down_weight_t, router.T, cluster_ids)
 
 
 def solution(mesh):

time: 130 us -> 120 us (0.923); the launches traced: 130 us -> 118 us
  Pallas kernels: 123 us -> 113 us
  local copies, waits for them, and re-layouts: 6.16 us -> 4.23 us
    pallas_call x1, Pallas kernels: 123 us -> 113 us  [per_device(): pl.pallas_call(kernel, out_shape=(jax.ShapeDtypeStruct((TOKENS // 128, D)...]
    unnamed x9 -> x2, local copies, waits for them, and re-layouts: 6.16 us -> 4.23 us
where the time goes in v2:
time: 120 us; the launch traced here: 118 us
  Pallas kernels  113 us (94%)
  local copies, waits for them, and re-layouts  4.23 us (4%)
    pallas_call x1, Pallas kernels, per_device(): pl.pallas_call(kernel, out_shape=(jax.ShapeDtypeStruct((TOKENS // 128, D)...  113 us
    unnamed x2, local copies, waits for them, and re-layouts  4.23 us

profile of v2, /device:TPU:1, one launch (start us, length us, event | category | flops | bytes accessed | tf_op | source)
XLA Modules:
  0.0 118.2 jit_solution(1367743007331933859)
XLA Ops:
  0.6 113.4 %shard_map.77 = (bf16[4,4096]{1,0:T(4,128)(2,1)}, bf16[32,28672]{1,0:T(8,128)(2,1)}) custom-call(bf16[4,4096]{1,0:T(4,128)(2,1)} %tok_in.1, bf16[32,28672]{1,0:T(8,128)(2,1)} %gw.1, bf16[32,28672]{1,0:T(8,128)(2,1)} %uw.1, bf16[32,28672]{1,0:T(8,128)(2,1)} %dw.1, bf16[16,4096]{1,0:T(8,128)(2,1)} %bitcast.1, s32[224]{0:T(256)} %ids.1), custom_call_target="tpu_custom_call" | custom-call | tf_op jit(solution)/shard_map/pallas_call | solution.py:342
  114.0 1.4 %copy.10 = bf16[4,4096]{1,0:T(4,128)(2,1)} copy(bf16[4,4096]{1,0:T(4,128)(2,1)} %get-tuple-element.4) | data formatting | bytes 65536
  115.4 2.8 %copy.11 = bf16[32,28672]{1,0:T(8,128)(2,1)} copy(bf16[32,28672]{1,0:T(8,128)(2,1)} %get-tuple-element.5) | data formatting | bytes 3670016

commit v3 on v2

--- a/solution.py
+++ b/solution.py
@@ -33,7 +33,17 @@
     ("P", 0, 1), ("P", 1, 1), ("H", 0), ("P", 0, 2), ("P", 1, 2), ("H", 1), ("F", 0),
     ("P", 0, 3), ("P", 1, 3), ("H", 2), ("F", 1), ("H", 3), ("F", 2), ("F", 3),
 )
+DOWN_CUTS = (((0, 896), (896, 896)), ((0, 896), (896, 896)))
+GRAD_CUTS = (((0, 896),), ((0, 896),))
 INV_ROOT = 1.0 / float(TOKENS) ** 0.5
+
+
+def div(a, b):
+    return lax.div(a, jnp.int32(b))
+
+
+def rem(a, b):
+    return lax.rem(a, jnp.int32(b))
 
 
 def local_copy(src, dst, sem):
@@ -52,11 +62,11 @@
 ):
     e = lax.axis_index("expert")
     d = lax.axis_index("dp")
-    y, c = e // 2, e % 2
-    x, z = d // 4, d % 4
+    y, c = div(e, 2), rem(e, 2)
+    x, z = div(d, 4), rem(d, 4)
 
     def plane_peer(o):
-        return ((x + o // 4) % 4) * 4 + (z + o % 4) % 4
+        return rem(x + div(o, 4), 4) * 4 + rem(z + rem(o, 4), 4)
 
     def remote(src, dst, ssem, rsem, te, td):
         pltpu.make_async_remote_copy(
@@ -81,16 +91,51 @@
 
     def greet_plane(o):
         pl.semaphore_signal(
-            bar, inc=1, device_id=(y * 2 + (c + o % 2) % 2, plane_peer(o // 2)), device_id_type=MESH
+            bar, inc=1, device_id=(y * 2 + rem(c + rem(o, 2), 2), plane_peer(div(o, 2))), device_id_type=MESH
         )
 
     each(1, 32, greet_plane)
 
     def greet_others(o):
-        y2 = (y + 1 + o // 2) % 4
-        pl.semaphore_signal(bar, inc=1, device_id=(y2 * 2 + o % 2, d), device_id_type=MESH)
+        y2 = rem(y + 1 + div(o, 2), 4)
+        pl.semaphore_signal(bar, inc=1, device_id=(y2 * 2 + rem(o, 2), d), device_id_type=MESH)
 
     each(0, 6, greet_others)
+
+    pl.semaphore_wait(bar, 37)
+
+    def issue_gu(m, k):
+        w = (gw, uw)[m]
+        n, first = CHUNKS[k], STARTS[k]
+        me = c * ND + d
+
+        def cols(c2, d2):
+            return pl.ds(pl.multiple_of(d2 * FD + c2 * FC + first * BLOCK, BLOCK), n * BLOCK)
+
+        def body(o):
+            c2, d2 = rem(c + rem(o, 2), 2), plane_peer(div(o, 2))
+            remote(w.at[:, cols(c2, d2)], wrecv[k].at[m, me], w_s.at[m, k], w_r.at[m, k], y * 2 + c2, d2)
+
+        each(1, 32, body)
+        local_copy(w.at[:, cols(c, d)], wrecv[k].at[m, me], w_r.at[m, k]).start()
+
+    def issue_down(h):
+        rows = pl.ds(h * RH, RH)
+        for first, width in DOWN_CUTS[h]:
+
+            def cols(d2):
+                return pl.ds(pl.multiple_of(d2 * FD + first, BLOCK), width)
+
+            to = wd.at[h, d, :, pl.ds(first, width)]
+
+            def body(o):
+                d2 = plane_peer(o)
+                remote(dw.at[rows, cols(d2)], to, d_s.at[h], d_r.at[h], e, d2)
+
+            each(1, ND, body)
+            local_copy(dw.at[rows, cols(d)], to, d_r.at[h]).start()
+
+    issue_gu(0, 0)
 
     tok_copy.wait()
     t = tok[...].astype(F32)
@@ -100,43 +145,11 @@
     for k in range(NY):
         tok_send[k] = t16[:, k * KD : (k + 1) * KD]
 
-    pl.semaphore_wait(bar, 37)
-
     def send_tok_col(o):
-        y2 = (y + o) % 4
+        y2 = rem(y + o, 4)
         remote(tok_send.at[y2], tok_recv.at[o - 1], tok_s.at[0], tok_s.at[1], y2 * 2 + c, d)
 
     each(1, NY, send_tok_col)
-
-    def issue_gu(m, k):
-        w = (gw, uw)[m]
-        n, first = CHUNKS[k], STARTS[k]
-        me = c * ND + d
-
-        def cols(c2, d2):
-            return pl.ds(pl.multiple_of(d2 * FD + c2 * FC + first * BLOCK, BLOCK), n * BLOCK)
-
-        def body(o):
-            c2, d2 = (c + o % 2) % 2, plane_peer(o // 2)
-            remote(w.at[:, cols(c2, d2)], wrecv[k].at[m, me], w_s.at[m, k], w_r.at[m, k], y * 2 + c2, d2)
-
-        each(1, 32, body)
-        local_copy(w.at[:, cols(c, d)], wrecv[k].at[m, me], w_r.at[m, k]).start()
-
-    def issue_down(h):
-        def cols(d2):
-            return pl.ds(pl.multiple_of(d2 * FD, BLOCK), FD)
-
-        rows = pl.ds(h * RH, RH)
-
-        def body(o):
-            d2 = plane_peer(o)
-            remote(dw.at[rows, cols(d2)], wd.at[h, d], d_s.at[h], d_r.at[h], e, d2)
-
-        each(1, ND, body)
-        local_copy(dw.at[rows, cols(d)], wd.at[h, d], d_r.at[h]).start()
-
-    issue_gu(0, 0)
 
     wait_bytes(tok_recv, tok_s.at[1])
     mine = tok_send[y].astype(F32)
@@ -166,7 +179,7 @@
         return pl.ds(pl.multiple_of(y2 * TQ, TQ), TQ)
 
     def send_logit(o):
-        y2 = (y + o) % 4
+        y2 = rem(y + o, 4)
         remote(logit.at[rows_of(y2)], lsum.at[o - 1], l_s, l_r, y2 * 2 + c, d)
 
     each(1, NY, send_logit)
@@ -183,7 +196,7 @@
             own[k][m][...] = dot
 
         def send(o):
-            y2 = (y + o) % 4
+            y2 = rem(y + o, 4)
             remote(part[k][m].at[rows_of(y2)], psum[k][m].at[o - 1], p_s.at[m, k], p_r.at[m, k], y2 * 2 + c, d)
 
         each(1, NY, send)
@@ -212,7 +225,7 @@
         view = s.at[c, rows_of(y), step_cols(k)]
 
         def send(o):
-            remote(view, view, s_s.at[k], s_r.at[k], (y + o) % 4 * 2 + c, d)
+            remote(view, view, s_s.at[k], s_r.at[k], rem(y + o, 4) * 2 + c, d)
 
         each(1, NY, send)
 
@@ -268,8 +281,8 @@
         each(1, ND, send)
 
         def send_out(o):
-            e2 = (e + o) % 8
-            rows = pl.ds(pl.multiple_of((e2 % 2) * 16, 16), 16)
+            e2 = rem(e + o, 8)
+            rows = pl.ds(pl.multiple_of(rem(e2, 2) * 16, 16), 16)
             remote(rfull.at[h, d, rows], out16.at[e, h], o_s.at[h], o_r.at[h], e2, d)
 
         each(1, 8, send_out)
@@ -279,18 +292,20 @@
     def gradient(h):
         wait_bytes(rfull.at[h, pl.ds(0, ND - 1)], ra_r.at[h])
         r = rfull[h].reshape(TOKENS, IH)
+        rows = pl.ds(h * RH, RH)
         for c2 in range(2):
             g = lax.dot_general(r, s[c2], (((0,), (0,)), ((), ())), preferred_element_type=F32)
             gs[h, :, :, c2 * FC : (c2 + 1) * FC] = (g * INV_ROOT).astype(BF).reshape(ND, RH, FC)
-        rows = pl.ds(h * RH, RH)
-        cols = pl.ds(pl.multiple_of(d * FD, BLOCK), FD)
-
-        def send(o):
-            d2 = plane_peer(o)
-            remote(gs.at[h, d2], grad_out.at[rows, cols], g_s.at[h], g_r.at[h], e, d2)
-
-        each(1, ND, send)
-        local_copy(gs.at[h, d], grad_out.at[rows, cols], g_r.at[h]).start()
+            for first, width in GRAD_CUTS[h]:
+                cols = pl.ds(pl.multiple_of(d * FD + c2 * FC + first, BLOCK), width)
+                part_cols = pl.ds(c2 * FC + first, width)
+
+                def send(o):
+                    d2 = plane_peer(o)
+                    remote(gs.at[h, d2, :, part_cols], grad_out.at[rows, cols], g_s.at[h], g_r.at[h], e, d2)
+
+                each(1, ND, send)
+                local_copy(gs.at[h, d, :, part_cols], grad_out.at[rows, cols], g_r.at[h]).start()
 
     residual(0)
     residual(1)
@@ -342,8 +357,8 @@
     return pl.pallas_call(
         kernel,
         out_shape=(
-            jax.ShapeDtypeStruct((TOKENS // 128, D), BF),
-            jax.ShapeDtypeStruct((ROWS, FF), BF),
+            pltpu.VMEM((TOKENS // 128, D), BF),
+            pltpu.VMEM((ROWS, FF), BF),
         ),
         in_specs=[hbm, hbm, hbm, hbm, hbm, smem],
         out_specs=(vmem, pl.BlockSpec(memory_space=pl.ANY)),

time: 120 us -> 114 us (0.950)
  local copies, waits for them, and re-layouts: 4.23 us -> 1.85 us
  Pallas kernels: 113 us -> 111 us
    pallas_call x1, Pallas kernels: 113 us -> 111 us  [per_device(): pl.pallas_call(kernel, out_shape=(pltpu.VMEM((TOKENS // 128, D), BF), plt...]
    unnamed x2, local copies, waits for them, and re-layouts: 4.23 us -> 1.85 us
where the time goes in v3:
time: 114 us; the launch traced here: 113 us
  Pallas kernels  111 us (97%)
  local copies, waits for them, and re-layouts  1.85 us (2%)
    pallas_call x1, Pallas kernels, per_device(): pl.pallas_call(kernel, out_shape=(pltpu.VMEM((TOKENS // 128, D), BF), plt...  111 us

profile of v3, /device:TPU:1, one launch (start us, length us, event | category | flops | bytes accessed | tf_op | source)
XLA Modules:
  0.0 113.0 jit_solution(9859163661084038366)
XLA Ops:
  0.6 110.5 %shard_map.77 = (bf16[4,4096]{1,0:T(4,128)(2,1)S(1)}, bf16[32,28672]{1,0:T(8,128)(2,1)S(1)}) custom-call(bf16[4,4096]{1,0:T(4,128)(2,1)} %tok_in.1, bf16[32,28672]{1,0:T(8,128)(2,1)} %gw.1, bf16[32,28672]{1,0:T(8,128)(2,1)} %uw.1, bf16[32,28672]{1,0:T(8,128)(2,1)} %dw.1, bf16[16,4096]{1,0:T(8,128)(2,1)} %bitcast.1, s32[224]{0:T(256)} %ids.1), custom_call_target="tpu_custom_call" | custom-call | tf_op jit(solution)/shard_map/pallas_call | solution.py:357
  111.1 0.6 copy.10
  111.8 1.2 %copy.11 = bf16[32,28672]{1,0:T(8,128)(2,1)} copy(bf16[32,28672]{1,0:T(8,128)(2,1)S(1)} %get-tuple-element.3) | data formatting | bytes 3670016

commit v4 on v3

--- a/solution.py
+++ b/solution.py
@@ -34,7 +34,11 @@
     ("P", 0, 3), ("P", 1, 3), ("H", 2), ("F", 1), ("H", 3), ("F", 2), ("F", 3),
 )
 DOWN_CUTS = (((0, 896), (896, 896)), ((0, 896), (896, 896)))
-GRAD_CUTS = (((0, 896),), ((0, 896),))
+GRAD_CUTS = ((((0, 256), (256, 640)), ((0, 896),)), (((0, 896),), ((0, 512), (512, 384))))
+OFFSETS = (
+    (2, 2), (2, 1), (2, 3), (1, 2), (3, 2), (2, 0), (0, 2), (1, 1),
+    (3, 3), (1, 3), (3, 1), (1, 0), (3, 0), (0, 1), (0, 3),
+)
 INV_ROOT = 1.0 / float(TOKENS) ** 0.5
 
 
@@ -66,7 +70,13 @@
     x, z = div(d, 4), rem(d, 4)
 
     def plane_peer(o):
+        if isinstance(o, tuple):
+            return rem(x + o[0], 4) * 4 + rem(z + o[1], 4)
         return rem(x + div(o, 4), 4) * 4 + rem(z + rem(o, 4), 4)
+
+    def each_peer(body):
+        for offset in OFFSETS:
+            body(offset)
 
     def remote(src, dst, ssem, rsem, te, td):
         pltpu.make_async_remote_copy(
@@ -79,6 +89,21 @@
             return carry
 
         lax.fori_loop(lo, hi, step, 0)
+
+    bar = pltpu.get_barrier_semaphore()
+
+    def greet_plane(o):
+        pl.semaphore_signal(
+            bar, inc=1, device_id=(y * 2 + rem(c + rem(o, 2), 2), plane_peer(div(o, 2))), device_id_type=MESH
+        )
+
+    each(1, 32, greet_plane)
+
+    def greet_others(o):
+        y2 = rem(y + 1 + div(o, 2), 4)
+        pl.semaphore_signal(bar, inc=1, device_id=(y2 * 2 + rem(o, 2), d), device_id_type=MESH)
+
+    each(0, 6, greet_others)
 
     tok_copy = local_copy(tok_in, tok, in_s.at[0])
     tok_copy.start()
@@ -87,21 +112,6 @@
     )
     router_copy.start()
 
-    bar = pltpu.get_barrier_semaphore()
-
-    def greet_plane(o):
-        pl.semaphore_signal(
-            bar, inc=1, device_id=(y * 2 + rem(c + rem(o, 2), 2), plane_peer(div(o, 2))), device_id_type=MESH
-        )
-
-    each(1, 32, greet_plane)
-
-    def greet_others(o):
-        y2 = rem(y + 1 + div(o, 2), 4)
-        pl.semaphore_signal(bar, inc=1, device_id=(y2 * 2 + rem(o, 2), d), device_id_type=MESH)
-
-    each(0, 6, greet_others)
-
     pl.semaphore_wait(bar, 37)
 
     def issue_gu(m, k):
@@ -113,10 +123,13 @@
             return pl.ds(pl.multiple_of(d2 * FD + c2 * FC + first * BLOCK, BLOCK), n * BLOCK)
 
         def body(o):
-            c2, d2 = rem(c + rem(o, 2), 2), plane_peer(div(o, 2))
+            c2, d2 = rem(c + o[2], 2), plane_peer(o[:2])
             remote(w.at[:, cols(c2, d2)], wrecv[k].at[m, me], w_s.at[m, k], w_r.at[m, k], y * 2 + c2, d2)
 
-        each(1, 32, body)
+        for other in range(2):
+            for offset in OFFSETS:
+                body(offset + (other,))
+        body((0, 0, 1))
         local_copy(w.at[:, cols(c, d)], wrecv[k].at[m, me], w_r.at[m, k]).start()
 
     def issue_down(h):
@@ -132,7 +145,7 @@
                 d2 = plane_peer(o)
                 remote(dw.at[rows, cols(d2)], to, d_s.at[h], d_r.at[h], e, d2)
 
-            each(1, ND, body)
+            each_peer(body)
             local_copy(dw.at[rows, cols(d)], to, d_r.at[h]).start()
 
     issue_gu(0, 0)
@@ -160,7 +173,7 @@
     def send_tok_plane(o):
         remote(tokens.at[d, c], tokens.at[d, c], tok_s.at[2], tok_s.at[3], e, plane_peer(o))
 
-    each(1, ND, send_tok_plane)
+    each_peer(send_tok_plane)
     issue_gu(1, 0)
     issue_gu(0, 1)
     wait_bytes(tokens.at[pl.ds(0, ND - 1), 0], tok_s.at[3])
@@ -263,9 +276,9 @@
 
         def send(o):
             d2 = plane_peer(o)
-            remote(p.at[h, d2], rr.at[h, o - 1], rp_s.at[h], rp_r.at[h], e, d2)
-
-        each(1, ND, send)
+            remote(p.at[h, d2], rr.at[h, OFFSETS.index(o)], rp_s.at[h], rp_r.at[h], e, d2)
+
+        each_peer(send)
 
     def reduce_residual(h):
         wait_bytes(rr.at[h], rp_r.at[h])
@@ -278,8 +291,9 @@
         def send(o):
             remote(view, view, ra_s.at[h], ra_r.at[h], e, plane_peer(o))
 
-        each(1, ND, send)
-
+        each_peer(send)
+
+    def send_rows(h):
         def send_out(o):
             e2 = rem(e + o, 8)
             rows = pl.ds(pl.multiple_of(rem(e2, 2) * 16, 16), 16)
@@ -294,17 +308,19 @@
         r = rfull[h].reshape(TOKENS, IH)
         rows = pl.ds(h * RH, RH)
         for c2 in range(2):
-            g = lax.dot_general(r, s[c2], (((0,), (0,)), ((), ())), preferred_element_type=F32)
-            gs[h, :, :, c2 * FC : (c2 + 1) * FC] = (g * INV_ROOT).astype(BF).reshape(ND, RH, FC)
-            for first, width in GRAD_CUTS[h]:
+            for first, width in GRAD_CUTS[h][c2]:
+                dot = lax.dot_general(
+                    r, s[c2, :, first : first + width], (((0,), (0,)), ((), ())), preferred_element_type=F32
+                )
                 cols = pl.ds(pl.multiple_of(d * FD + c2 * FC + first, BLOCK), width)
                 part_cols = pl.ds(c2 * FC + first, width)
+                gs[h, :, :, part_cols] = (dot * INV_ROOT).astype(BF).reshape(ND, RH, width)
 
                 def send(o):
                     d2 = plane_peer(o)
                     remote(gs.at[h, d2, :, part_cols], grad_out.at[rows, cols], g_s.at[h], g_r.at[h], e, d2)
 
-                each(1, ND, send)
+                each_peer(send)
                 local_copy(gs.at[h, d, :, part_cols], grad_out.at[rows, cols], g_r.at[h]).start()
 
     residual(0)
@@ -313,6 +329,8 @@
     reduce_residual(1)
     gradient(0)
     gradient(1)
+    send_rows(0)
+    send_rows(1)
 
     for h in range(H):
         wait_bytes(out16.at[:, h], o_r.at[h])

time: 114 us -> 112 us (0.982)
  Pallas kernels: 111 us -> 108 us
    pallas_call x1, Pallas kernels: 111 us -> 108 us  [per_device(): pl.pallas_call(kernel, out_shape=(pltpu.VMEM((TOKENS // 128, D), BF), plt...]
where the time goes in v4:
time: 112 us; the launch traced here: 111 us
  Pallas kernels  108 us (96%)
  local copies, waits for them, and re-layouts  1.85 us (2%)
    pallas_call x1, Pallas kernels, per_device(): pl.pallas_call(kernel, out_shape=(pltpu.VMEM((TOKENS // 128, D), BF), plt...  108 us

profile of v4, /device:TPU:1, one launch (start us, length us, event | category | flops | bytes accessed | tf_op | source)
XLA Modules:
  0.0 110.9 jit_solution(14627265458401814463)
XLA Ops:
  0.6 108.4 %shard_map.77 = (bf16[4,4096]{1,0:T(4,128)(2,1)S(1)}, bf16[32,28672]{1,0:T(8,128)(2,1)S(1)}) custom-call(bf16[4,4096]{1,0:T(4,128)(2,1)} %tok_in.1, bf16[32,28672]{1,0:T(8,128)(2,1)} %gw.1, bf16[32,28672]{1,0:T(8,128)(2,1)} %uw.1, bf16[32,28672]{1,0:T(8,128)(2,1)} %dw.1, bf16[16,4096]{1,0:T(8,128)(2,1)} %bitcast.1, s32[224]{0:T(256)} %ids.1), custom_call_target="tpu_custom_call" | custom-call | tf_op jit(solution)/shard_map/pallas_call | solution.py:375
  109.0 0.6 copy.10
  109.7 1.2 %copy.11 = bf16[32,28672]{1,0:T(8,128)(2,1)} copy(bf16[32,28672]{1,0:T(8,128)(2,1)S(1)} %get-tuple-element.3) | data formatting | bytes 3670016

commit v5 on v4

--- a/solution.py
+++ b/solution.py
@@ -112,44 +112,6 @@
     )
     router_copy.start()
 
-    pl.semaphore_wait(bar, 37)
-
-    def issue_gu(m, k):
-        w = (gw, uw)[m]
-        n, first = CHUNKS[k], STARTS[k]
-        me = c * ND + d
-
-        def cols(c2, d2):
-            return pl.ds(pl.multiple_of(d2 * FD + c2 * FC + first * BLOCK, BLOCK), n * BLOCK)
-
-        def body(o):
-            c2, d2 = rem(c + o[2], 2), plane_peer(o[:2])
-            remote(w.at[:, cols(c2, d2)], wrecv[k].at[m, me], w_s.at[m, k], w_r.at[m, k], y * 2 + c2, d2)
-
-        for other in range(2):
-            for offset in OFFSETS:
-                body(offset + (other,))
-        body((0, 0, 1))
-        local_copy(w.at[:, cols(c, d)], wrecv[k].at[m, me], w_r.at[m, k]).start()
-
-    def issue_down(h):
-        rows = pl.ds(h * RH, RH)
-        for first, width in DOWN_CUTS[h]:
-
-            def cols(d2):
-                return pl.ds(pl.multiple_of(d2 * FD + first, BLOCK), width)
-
-            to = wd.at[h, d, :, pl.ds(first, width)]
-
-            def body(o):
-                d2 = plane_peer(o)
-                remote(dw.at[rows, cols(d2)], to, d_s.at[h], d_r.at[h], e, d2)
-
-            each_peer(body)
-            local_copy(dw.at[rows, cols(d)], to, d_r.at[h]).start()
-
-    issue_gu(0, 0)
-
     tok_copy.wait()
     t = tok[...].astype(F32)
     t16 = jnp.concatenate([t] * 4, axis=0)
@@ -158,11 +120,50 @@
     for k in range(NY):
         tok_send[k] = t16[:, k * KD : (k + 1) * KD]
 
+    pl.semaphore_wait(bar, 37)
+
     def send_tok_col(o):
         y2 = rem(y + o, 4)
         remote(tok_send.at[y2], tok_recv.at[o - 1], tok_s.at[0], tok_s.at[1], y2 * 2 + c, d)
 
     each(1, NY, send_tok_col)
+
+
+    def issue_gu(m, k):
+        w = (gw, uw)[m]
+        n, first = CHUNKS[k], STARTS[k]
+        me = c * ND + d
+
+        def cols(c2, d2):
+            return pl.ds(pl.multiple_of(d2 * FD + c2 * FC + first * BLOCK, BLOCK), n * BLOCK)
+
+        def body(o):
+            c2, d2 = rem(c + o[2], 2), plane_peer(o[:2])
+            remote(w.at[:, cols(c2, d2)], wrecv[k].at[m, me], w_s.at[m, k], w_r.at[m, k], y * 2 + c2, d2)
+
+        for other in range(2):
+            for offset in OFFSETS:
+                body(offset + (other,))
+        body((0, 0, 1))
+        local_copy(w.at[:, cols(c, d)], wrecv[k].at[m, me], w_r.at[m, k]).start()
+
+    def issue_down(h):
+        rows = pl.ds(h * RH, RH)
+        for first, width in DOWN_CUTS[h]:
+
+            def cols(d2):
+                return pl.ds(pl.multiple_of(d2 * FD + first, BLOCK), width)
+
+            to = wd.at[h, d, :, pl.ds(first, width)]
+
+            def body(o):
+                d2 = plane_peer(o)
+                remote(dw.at[rows, cols(d2)], to, d_s.at[h], d_r.at[h], e, d2)
+
+            each_peer(body)
+            local_copy(dw.at[rows, cols(d)], to, d_r.at[h]).start()
+
+    issue_gu(0, 0)
 
     wait_bytes(tok_recv, tok_s.at[1])
     mine = tok_send[y].astype(F32)

time: 112 us -> 112 us (level)
  no operation moved by 1% of the time
where the time goes in v5:
time: 112 us; the launch traced here: 111 us
  Pallas kernels  109 us (97%)
  local copies, waits for them, and re-layouts  1.85 us (2%)
    pallas_call x1, Pallas kernels, per_device(): pl.pallas_call(kernel, out_shape=(pltpu.VMEM((TOKENS // 128, D), BF), plt...  109 us

profile of v5, /device:TPU:1, one launch (start us, length us, event | category | flops | bytes accessed | tf_op | source)
XLA Modules:
  0.0 111.4 jit_solution(3356747692652948811)
XLA Ops:
  0.6 109.0 %shard_map.77 = (bf16[4,4096]{1,0:T(4,128)(2,1)S(1)}, bf16[32,28672]{1,0:T(8,128)(2,1)S(1)}) custom-call(bf16[4,4096]{1,0:T(4,128)(2,1)} %tok_in.1, bf16[32,28672]{1,0:T(8,128)(2,1)} %gw.1, bf16[32,28672]{1,0:T(8,128)(2,1)} %uw.1, bf16[32,28672]{1,0:T(8,128)(2,1)} %dw.1, bf16[16,4096]{1,0:T(8,128)(2,1)} %bitcast.1, s32[224]{0:T(256)} %ids.1), custom_call_target="tpu_custom_call" | custom-call | tf_op jit(solution)/shard_map/pallas_call | solution.py:376
  109.6 0.6 copy.10
  110.2 1.2 %copy.11 = bf16[32,28672]{1,0:T(8,128)(2,1)} copy(bf16[32,28672]{1,0:T(8,128)(2,1)S(1)} %get-tuple-element.3) | data formatting | bytes 3670016
